TPU v7x, 32 devices: a whole 2x2x4 slice. The times are simulated.
32 devices in a mesh: seq: 4 (over z), row: 2 (over core), col: 4 (over y, x).
Axes of the slice: x: 2, y: 2, z: 4, core: 2. Of those that a mesh axis runs over, the one named last changes fastest.
Arguments:
- tokens: bfloat16 [512, 4096], P('seq', 'row'), may hold values from -40 to 40
- block_order: int32 [8], replicated, may hold values from 0 to 7, as said below
- query_weight: bfloat16 [4096, 4096], P('row', 'col'), may hold values from -0.09375 to 0.09375
- key_weight: bfloat16 [4096, 1024], P('row', 'col'), may hold values from -0.09375 to 0.09375
- value_weight: bfloat16 [4096, 1024], P('row', 'col'), may hold values from -0.09375 to 0.09375
- output_weight: bfloat16 [4096, 4096], P('col'), may hold values from -0.09375 to 0.09375
Outputs:
- layer_out: float32 [512, 4096], P('seq', ('row', 'col'))
Inputs may be any that keep to these rules, and one draw needn't show every extreme that they name: Slots 2 d and 2 d + 1 are the rows of device d along seq; for every d, block_order[2 d + 1] = 7 - block_order[2 d] with block_order[2 d] < 4, and every half-block appears once.
All inputs are finite; a program needn't handle non-finite values.
Results may differ from a plain program's by a relative error of at most 0.012.
The roundings to bfloat16 on the way count: a program that leaves them out, or rounds other values in their place, can miss the bound.
Values may be sent and summed in bfloat16 or wider, within the bound.
A program may use at most 64 MiB of HBM per device.

v0:
```python
from functools import partial

import jax
import jax.numpy as jnp
from jax import lax
from jax.sharding import PartitionSpec as P

H = 32
KV = 8
HD = 128


rope_theta = 500000.0
large_negative = -1e30


def shifted(array, axis, by):
    peers = lax.axis_size(axis)
    return lax.ppermute(array, axis, [(i, (i + by) % peers) for i in range(peers)])


def rotate(vectors, positions):
    half_width = vectors.shape[-1] // 2
    freqs = rope_theta ** (-(jnp.arange(half_width, dtype=jnp.float32) * 2.0 / vectors.shape[-1]))
    angles = positions.astype(jnp.float32)[:, None] * freqs[None, :]
    cosine = jnp.cos(angles)[:, None, :]
    sine = jnp.sin(angles)[:, None, :]
    first = vectors[..., :half_width]
    second = vectors[..., half_width:]
    return jnp.concatenate(
        [first * cosine - second * sine, second * cosine + first * sine], axis=-1
    )


def token_positions(block_order, first_row, count, half_rows):
    rows_index = first_row + jnp.arange(count, dtype=jnp.int32)
    slots = rows_index // half_rows
    matched = slots[:, None] == jnp.arange(block_order.shape[0], dtype=jnp.int32)[None, :]
    chosen = jnp.sum(jnp.where(matched, block_order[None, :], 0), axis=1)
    return chosen * half_rows + rows_index % half_rows


def attend_block(queries, query_pos, carry_state, key_values, key_pos):
    highest, denom, accum = carry_state
    scores = jnp.einsum("qhd,kd->qhk", queries, key_values[0], preferred_element_type=jnp.float32)
    scores = scores * queries.shape[-1] ** (-0.5)
    visible = key_pos[None, None, :] <= query_pos[:, None, None]
    scores = jnp.where(visible, scores, large_negative)
    new_highest = jnp.maximum(highest, jnp.max(scores, axis=-1))
    rescale = jnp.exp(highest - new_highest)
    weights = jnp.where(visible, jnp.exp(scores - new_highest[..., None]), 0.0)
    denom = denom * rescale + jnp.sum(weights, axis=-1)
    mixed = jnp.einsum(
        "qhk,kd->qhd",
        weights.astype(jnp.bfloat16),
        key_values[1],
        preferred_element_type=jnp.float32,
    )
    accum = accum * rescale[..., None] + mixed
    return (new_highest, denom, accum)


def body(tokens, block_order, query_weight, key_weight, value_weight, output_weight):
    rows_here = tokens.shape[0]
    half_rows = rows_here // 2
    seq_count = lax.axis_size("seq")
    seq_index = lax.axis_index("seq")
    row_index = lax.axis_index("row")
    head_width = HD
    query_part = jnp.dot(tokens, query_weight, preferred_element_type=jnp.float32)
    queries = lax.psum_scatter(query_part, "row", scatter_dimension=1, tiled=True)
    keys_part = jnp.dot(tokens, key_weight, preferred_element_type=jnp.float32)
    values_part = jnp.dot(tokens, value_weight, preferred_element_type=jnp.float32)
    keys_summed, values_summed = lax.psum((keys_part, values_part), "row")
    heads_here = queries.shape[1] // head_width
    group_size = H // KV
    kv_local = row_index * heads_here // group_size
    own_pos = token_positions(block_order, seq_index * rows_here, rows_here, half_rows)
    queries = rotate(queries.reshape(rows_here, heads_here, head_width), own_pos).astype(
        jnp.bfloat16
    )
    attend = partial(attend_block, queries, own_pos)
    carry_state = (
        jnp.full((rows_here, heads_here), large_negative, jnp.float32),
        jnp.zeros((rows_here, heads_here), jnp.float32),
        jnp.zeros((rows_here, heads_here, head_width), jnp.float32),
    )

    def source_positions(source):
        return token_positions(block_order, source * rows_here, rows_here, half_rows)

    key_one = lax.dynamic_slice_in_dim(keys_summed, kv_local * head_width, head_width, 1)
    value_one = lax.dynamic_slice_in_dim(values_summed, kv_local * head_width, head_width, 1)
    key_one = rotate(key_one[:, None, :], own_pos)[:, 0, :].astype(jnp.bfloat16)
    key_values = jnp.stack([key_one, value_one.astype(jnp.bfloat16)])
    carry_state = attend(carry_state, key_values, own_pos)

    def beside_all(shift_count, loop_carry):
        carry_now, travelling = loop_carry
        travelling = shifted(travelling, "seq", 1)
        source = (seq_index - shift_count) % seq_count
        carry_now = attend(carry_now, travelling, source_positions(source))
        return (carry_now, travelling)

    carry_state, unused = lax.fori_loop(1, seq_count, beside_all, (carry_state, key_values))
    highest, denom, accum = carry_state
    attended = (
        (accum / denom[..., None]).astype(jnp.bfloat16).reshape(rows_here, heads_here * head_width)
    )
    out_rows = lax.dynamic_slice_in_dim(
        output_weight, row_index * heads_here * head_width, heads_here * head_width, 0
    )
    partial_out = jnp.dot(attended, out_rows, preferred_element_type=jnp.float32)
    return lax.psum_scatter(partial_out, ("row", "col"), scatter_dimension=1, tiled=True)


def solution(mesh):
    placed = (
        P("seq", "row"),
        P(),
        P("row", "col"),
        P("row", "col"),
        P("row", "col"),
        P("col", None),
    )
    return jax.shard_map(
        body, mesh=mesh, in_specs=placed, out_specs=P("seq", ("row", "col")), check_vma=False
    )
```

profile of v0, /device:TPU:0, one launch (start us, length us, event | category | flops | bytes accessed | tf_op | source)
XLA Modules:
  0.0 115.1 jit_solution(6260908952147884425)
XLA Ops:
  6.6 1.2 %copy-done = bf16[2048,256]{1,0:T(8,128)(2,1)S(1)} copy-done((bf16[2048,256]{1,0:T(8,128)(2,1)S(1)}, bf16[2048,256]{1,0:T(8,128)(2,1)}, u32[]{:S(2)}) %copy-start) | copy-done | bytes 1048600
  7.8 2.0 %fusion.39 = f32[128,256]{1,0:T(8,128)} fusion(bf16[128,2048]{1,0:T(8,128)(2,1)} %param.8, bf16[2048,256]{1,0:T(8,128)(2,1)S(1)} %copy-done), kind=kOutput, calls=%fused_computation.79 | convolution fusion | flops 134217728 | bytes 1703936 | tf_op jit(solution)/shard_map/dot_general | solution.py:72
  9.9 3.9 %fusion.38 = f32[128,1024]{1,0:T(8,128)} fusion(bf16[128,2048]{1,0:T(8,128)(2,1)} %param.8, bf16[2048,1024]{1,0:T(8,128)(2,1)} %param.10), kind=kOutput, calls=%fused_computation.78 | convolution fusion | flops 536870912 | bytes 5242880 | tf_op jit(solution)/shard_map/dot_general | solution.py:70
  14.0 0.3 fusion.40
  14.3 4.2 %all-reduce.4 = bf16[128,256]{1,0:T(8,128)(2,1)S(1)} all-reduce(f32[128,256]{1,0:T(8,128)S(1)} %fusion.40), channel_id=1, replica_groups=mesh['seq'=4,'row'=2,'col'=4] {'row'}, use_global_device_ids=true, to_apply=%region_5.6 | all-reduce | flops 32768 | bytes 196608 | tf_op jit(solution)/shard_map/psum | solution.py:74
  18.6 0.3 multiply_cosine_fusion.1
  18.9 11.7 %all-reduce.3.cloned.1.call-done = f32[128,256]{1,0:T(8,128)} async-done(((f32[128,256]{1,0:T(8,128)}), f32[128,256]{1,0:T(8,128)}) %all-reduce.3.cloned.1.call-update) | async-done | bytes 131088 | tf_op jit(solution)/shard_map/psum | solution.py:74
  30.6 0.8 dynamic-slice_bitcast_fusion
  31.4 0.3 fusion.22
  31.9 10.1 %reduce-scatter.3.cloned.1.call-done = f32[128,512]{1,0:T(8,128)} async-done(((f32[128,1024]{1,0:T(8,128)}), f32[128,512]{1,0:T(8,128)}) %reduce-scatter.3.cloned.1.call-update) | async-done | bytes 262160 | tf_op jit(solution)/shard_map/reduce_scatter | solution.py:71
  42.0 1.0 reshape.302
  43.0 0.2 fusion.35
  43.3 0.1 pad_maximum_fusion
  43.4 0.2 fusion.36
  43.8 0.2 convolution_add_fusion.1
  44.0 20.3 %while.22 = (s32[]{:T(128)}, f32[128,4]{0,1:T(4,128)S(1)}, f32[128,4]{0,1:T(4,128)S(1)}, f32[128,4,128]{2,0,1:T(8,128)S(1)}, bf16[2,128,128]{2,1,0:T(8,128)(2,1)...) while((s32[]{:T(128)}, f32[128,4]{0,1:T(4,128)S(1)}, ...), condition=%wide.region_10.11_spmd, body=%wide.region_6.10_spmd.sunk | while | flops 34299536 | bytes 2002778 | solution.py:105
  44.0 1.8 %collective-permute-start = (bf16[2,128,128]{2,1,0:T(8,128)(2,1)S(1)}, bf16[2,128,128]{2,1,0:T(8,128)(2,1)S(1)}, u32[]{:S(2)}, u32[]{:S(2)}) collective-permute-start(bf16[2,128,128]{2,1,0:T(8,128)(2,1)S(1)} %get-tuple-element.381), channel_id=1, source_target_pairs={{0,8},{8,16},{16,24},{24,0},{1,9},{9,17},{17,25},{25,1},{2,10},{10... | collective-permute-start | bytes 196616 | tf_op jit(solution)/shard_map/while/body/eval_jaxpr/ppermute | solution.py:19
  45.9 0.1 broadcast_compare_fusion.3
  46.0 4.2 %collective-permute-done = bf16[2,128,128]{2,1,0:T(8,128)(2,1)S(1)} collective-permute-done((bf16[2,128,128]{2,1,0:T(8,128)(2,1)S(1)}, bf16[2,128,128]{2,1,0:T(8,128)(2,1)S(1)}, u32[]{:S(2)}, u32[]{:S(2)}) %collective-permute-start) | collective-permute-done | bytes 65568 | tf_op jit(solution)/shard_map/while/body/eval_jaxpr/ppermute | solution.py:19
  50.2 0.2 fusion.58
  50.5 0.3 convolution_add_fusion.3
  51.0 0.1 broadcast_compare_fusion.3
  51.1 5.8 %collective-permute-done = bf16[2,128,128]{2,1,0:T(8,128)(2,1)S(1)} collective-permute-done((bf16[2,128,128]{2,1,0:T(8,128)(2,1)S(1)}, bf16[2,128,128]{2,1,0:T(8,128)(2,1)S(1)}, u32[]{:S(2)}, u32[]{:S(2)}) %collective-permute-start) | collective-permute-done | bytes 65568 | tf_op jit(solution)/shard_map/while/body/eval_jaxpr/ppermute | solution.py:19
  57.0 0.2 fusion.58
  57.3 0.3 convolution_add_fusion.3
  57.8 0.1 broadcast_compare_fusion.3
  57.9 5.8 %collective-permute-done = bf16[2,128,128]{2,1,0:T(8,128)(2,1)S(1)} collective-permute-done((bf16[2,128,128]{2,1,0:T(8,128)(2,1)S(1)}, bf16[2,128,128]{2,1,0:T(8,128)(2,1)S(1)}, u32[]{:S(2)}, u32[]{:S(2)}) %collective-permute-start) | collective-permute-done | bytes 65568 | tf_op jit(solution)/shard_map/while/body/eval_jaxpr/ppermute | solution.py:19
  63.7 0.2 fusion.58
  64.0 0.3 convolution_add_fusion.3
  64.3 0.1 copy.20
  64.5 4.3 %fusion.9 = f32[128,4096]{1,0:T(8,128)} fusion(bf16[128,512]{0,1:T(8,128)(2,1)S(1)} %bitcast.41, bf16[1024,4096]{1,0:T(8,128)(2,1)} %param.13, s32[]{:T(128)S(6)} %select_n.147), kind=kOutput, calls=%fused_computation.24 | convolution fusion | flops 536870912 | bytes 6422532 | tf_op jit(solution)/shard_map/dot_general | solution.py:113
  68.8 39.7 %reduce-scatter.5.cloned.1.call-done = f32[128,512]{1,0:T(8,128)} async-done(((f32[128,4096]{1,0:T(8,128)}), f32[128,512]{1,0:T(8,128)}) %reduce-scatter.5.cloned.1.call-update) | async-done | bytes 262160 | tf_op jit(solution)/shard_map/reduce_scatter | solution.py:114
  (52 shorter events, 1.4 us)
Async XLA Ops:
  6.5 1.2 %copy-start = (bf16[2048,256]{1,0:T(8,128)(2,1)S(1)}, bf16[2048,256]{1,0:T(8,128)(2,1)}, u32[]{:S(2)}) copy-start(bf16[2048,256]{1,0:T(8,128)(2,1)} %param.11) | copy-start | bytes 3145732
  6.5 7.4 %copy-start.1 = (bf16[128,2048]{1,0:T(8,128)(2,1)S(1)}, bf16[128,2048]{1,0:T(8,128)(2,1)}, u32[]{:S(2)}) copy-start(bf16[128,2048]{1,0:T(8,128)(2,1)} %param.8) | copy-start | bytes 1572868
  6.5 7.3 %copy-start.3 = (s32[8]{0:T(128)S(1)}, s32[8]{0:T(128)}, u32[]{:S(2)}) copy-start(s32[8]{0:T(128)} %param.9) | copy-start | bytes 100
  6.5 7.4 %copy-start.2 = (bf16[2048,256]{1,0:T(8,128)(2,1)S(1)}, bf16[2048,256]{1,0:T(8,128)(2,1)}, u32[]{:S(2)}) copy-start(bf16[2048,256]{1,0:T(8,128)(2,1)} %param.12) | copy-start | bytes 3145732
  6.5 24.0 %all-reduce.3.cloned.1.call-start = ((), (), s32[]{:S(2)}) async-start(), calls=%async_computation.3 | async-start | bytes 262144 | tf_op jit(solution)/shard_map/psum | solution.py:74
  9.8 32.2 %reduce-scatter.3.cloned.1.call-start = ((), (), s32[]{:S(2)}) async-start(), calls=%async_computation.2 | async-start | bytes 786432 | tf_op jit(solution)/shard_map/reduce_scatter | solution.py:71
  13.7 94.8 %reduce-scatter.5.cloned.1.call-start = ((), (), s32[]{:S(2)}) async-start(), calls=%async_computation.4 | async-start | bytes 2359296 | tf_op jit(solution)/shard_map/reduce_scatter | solution.py:114
  44.0 6.2 %collective-permute-start = (bf16[2,128,128]{2,1,0:T(8,128)(2,1)S(1)}, bf16[2,128,128]{2,1,0:T(8,128)(2,1)S(1)}, u32[]{:S(2)}, u32[]{:S(2)}) collective-permute-start(bf16[2,128,128]{2,1,0:T(8,128)(2,1)S(1)} %get-tuple-element.381), channel_id=1, source_target_pairs={{0,8},{8,16},{16,24},{24,0},{1,9},{9,17},{17,25},{25,1},{2,10},{10... | collective-permute-start | bytes 196616 | tf_op jit(solution)/shard_map/while/body/eval_jaxpr/ppermute | solution.py:19
  50.8 6.1 %collective-permute-start = (bf16[2,128,128]{2,1,0:T(8,128)(2,1)S(1)}, bf16[2,128,128]{2,1,0:T(8,128)(2,1)S(1)}, u32[]{:S(2)}, u32[]{:S(2)}) collective-permute-start(bf16[2,128,128]{2,1,0:T(8,128)(2,1)S(1)} %get-tuple-element.381), channel_id=1, source_target_pairs={{0,8},{8,16},{16,24},{24,0},{1,9},{9,17},{17,25},{25,1},{2,10},{10... | collective-permute-start | bytes 196616 | tf_op jit(solution)/shard_map/while/body/eval_jaxpr/ppermute | solution.py:19
  57.6 6.1 %collective-permute-start = (bf16[2,128,128]{2,1,0:T(8,128)(2,1)S(1)}, bf16[2,128,128]{2,1,0:T(8,128)(2,1)S(1)}, u32[]{:S(2)}, u32[]{:S(2)}) collective-permute-start(bf16[2,128,128]{2,1,0:T(8,128)(2,1)S(1)} %get-tuple-element.381), channel_id=1, source_target_pairs={{0,8},{8,16},{16,24},{24,0},{1,9},{9,17},{17,25},{25,1},{2,10},{10... | collective-permute-start | bytes 196616 | tf_op jit(solution)/shard_map/while/body/eval_jaxpr/ppermute | solution.py:19
Sparse Core Ops, SparseCore 0:
  9.9 20.6 all-reduce.2
  32.8 9.1 reduce-scatter.2
  68.9 39.5 reduce-scatter.4
where the time goes:
time: 115 us
  waiting for transfers between devices  77.5 us (67%)
  between operations  13.3 us (12%)
  matrix products  12.4 us (11%)
  blocking collectives  4.15 us (4%)
  local copies, waits for them, and re-layouts  3.45 us (3%)
  other arithmetic  2.07 us (2%)
  starting transfers between devices  2 us (2%)
    reduce_scatter x1, waiting for transfers between devices, body(): lax.psum_scatter(partial_out, ('row', 'col'), scatter_dimension=1, tiled=...  39.7 us
    ppermute x3, waiting for transfers between devices, shifted(): lax.ppermute(array, axis, [(i, (i + by) % peers) for i in range(peers)])  15.9 us
    psum x1, waiting for transfers between devices, body(): keys_summed, values_summed = lax.psum((keys_part, values_part), 'row')  11.7 us
    reduce_scatter x1, waiting for transfers between devices, body(): lax.psum_scatter(query_part, 'row', scatter_dimension=1, tiled=True)  10.1 us
    dot_general x1, matrix products, body(): jnp.dot(attended, out_rows, preferred_element_type=jnp.float32)  4.3 us
    psum x1, blocking collectives, body(): keys_summed, values_summed = lax.psum((keys_part, values_part), 'row')  4.15 us
    dot_general x1, matrix products, body(): jnp.dot(tokens, query_weight, preferred_element_type=jnp.float32)  3.86 us
  transfers between devices with their start and end apart: 6, of which 6 were waited for; matrix products, arithmetic and copies ran while one was open for 6% of the time, Pallas kernels for 0%

commit v1 on v0

v1 whole, which is shorter than its diff:
```python
from functools import partial

import jax
import jax.numpy as jnp
import numpy as np
from jax import lax
from jax.experimental import pallas as pl
from jax.experimental.pallas import tpu as pltpu
from jax.sharding import PartitionSpec as P

H = 32
KV = 8
HD = 128
THETA = 500000.0
HIDDEN = -1e30
WIDE = 256
F32 = jnp.float32
BF16 = jnp.bfloat16


def rotary_table(half_rows, blocks):
    freqs = THETA ** (-2.0 * np.arange(HD // 2) / HD)
    starts = np.concatenate([np.arange(half_rows), half_rows * np.arange(blocks)])
    angles = starts[:, None] * freqs[None, :]
    cosine, sine = np.cos(angles), np.sin(angles)
    return np.concatenate([cosine, cosine, -sine, sine], axis=1).astype(np.float32)


def each(first, last, step):
    if last - first <= 8:
        for index in range(first, last):
            step(index)
    else:
        lax.fori_loop(first, last, lambda index, _: (step(index), 0)[1], 0)


def layer_kernel(
    seqs, cols,
    order_ref, x_hbm, wq_hbm, wk_hbm, wv_hbm, wo_hbm, table_hbm,
    out_ref,
    x, wkv, wq, wo, table, rot,
    kv_snd, kv_rcv, q_snd, q_rcv, q, kv, scores, att, att_peer, partial_own, rs_snd, rs_rcv,
    load_sem, wo_sem, core_send, core_recv, seq_send, seq_recv, col_send, col_recv,
):
    rows = x.shape[0]
    half = rows // 2
    heads = wq.shape[1] // 2 // HD
    width = heads * HD
    group = H // KV
    out_width = wo.shape[2]

    me_seq = lax.axis_index("seq")
    me_row = lax.axis_index("row")
    me_col = lax.axis_index("col")
    other = 1 - me_row

    def kv_columns(row):
        return pl.ds(pl.multiple_of(row * heads // group * HD, HD), HD)

    def q_columns(row):
        return pl.ds(pl.multiple_of(row * width, width), width)

    loads = [pltpu.make_async_copy(x_hbm, x, load_sem.at[0])]
    for slot, (source, row) in enumerate(
        [(wk_hbm, other), (wv_hbm, other), (wk_hbm, me_row), (wv_hbm, me_row)]
    ):
        loads.append(
            pltpu.make_async_copy(
                source.at[:, kv_columns(row)],
                wkv.at[:, pl.ds(slot * HD, HD)],
                load_sem.at[1 + slot],
            )
        )
    loads.append(pltpu.make_async_copy(table_hbm, table, load_sem.at[7]))
    for slot, row in enumerate([other, me_row]):
        loads.append(
            pltpu.make_async_copy(
                wq_hbm.at[:, q_columns(row)],
                wq.at[:, pl.ds(slot * width, width)],
                load_sem.at[5 + slot],
            )
        )
    for load in loads:
        load.start()
    load_x, load_kv, load_table, load_q = loads[0], loads[1:5], loads[5], loads[6:]

    def wo_load(step, part):
        target = lax.rem(me_col + step, cols)
        row = me_row if part == 0 else other
        first = pl.multiple_of((me_row * cols + target) * out_width, out_width)
        return pltpu.make_async_copy(
            wo_hbm.at[q_columns(row), pl.ds(first, out_width)],
            wo.at[step, pl.ds(part * width, width), :],
            wo_sem.at[step, part],
        )

    for part in range(2):
        for step in list(range(1, cols)) + [0]:
            wo_load(step, part).start()

    barrier = pltpu.get_barrier_semaphore()
    pl.semaphore_signal(barrier, inc=1, device_id={"row": other})
    each(1, seqs, lambda d: pl.semaphore_signal(
        barrier, inc=1, device_id={"seq": lax.rem(me_seq + d, seqs)}))
    each(1, cols, lambda d: pl.semaphore_signal(
        barrier, inc=1, device_id={"col": lax.rem(me_col + d, cols)}))

    load_table.wait()
    for part in range(2):
        cos_in = table[0:half, 0:HD]
        sin_in = table[0:half, HD:]
        start = table[pl.ds(half + order_ref[2 * me_seq + part], 1), :]
        cos_at, sin_at = start[:, :HD], start[:, HD:]
        here = pl.ds(part * half, half)
        rot[0, here, :] = cos_at * cos_in - sin_at * sin_in
        rot[1, here, :] = sin_at * cos_in + cos_at * sin_in

    def rotate(vectors):
        return vectors * rot[0] + pltpu.roll(vectors, HD // 2, 1) * rot[1]

    def to_core(source, target, index):
        return pltpu.make_async_remote_copy(
            src_ref=source, dst_ref=target,
            send_sem=core_send.at[index], recv_sem=core_recv.at[index],
            device_id={"row": other},
        )

    load_x.wait()
    load_kv[0].wait()
    load_kv[1].wait()
    kv_snd[...] = jnp.dot(x[...], wkv[:, : 2 * HD], preferred_element_type=F32).astype(kv_snd.dtype)
    pl.semaphore_wait(barrier, 1 + (seqs - 1) + (cols - 1))
    send_kv = to_core(kv_snd, kv_rcv, 0)
    send_kv.start()
    load_kv[2].wait()
    load_kv[3].wait()
    kv_own = jnp.dot(x[...], wkv[:, 2 * HD :], preferred_element_type=F32)
    send_kv.wait_recv()
    kv_sum = kv_own + kv_rcv[...].astype(F32)
    kv[me_seq, 0] = rotate(kv_sum[:, :HD]).astype(BF16)
    kv[me_seq, 1] = kv_sum[:, HD:].astype(BF16)

    def to_seq(d):
        return pltpu.make_async_remote_copy(
            src_ref=kv.at[me_seq], dst_ref=kv.at[me_seq],
            send_sem=seq_send.at[d], recv_sem=seq_recv.at[d],
            device_id={"seq": lax.rem(me_seq + d, seqs)},
        )

    def from_seq(d):
        source = lax.rem(me_seq - d + seqs, seqs)
        return pltpu.make_async_remote_copy(
            src_ref=kv.at[source], dst_ref=kv.at[source],
            send_sem=seq_send.at[d], recv_sem=seq_recv.at[d],
            device_id={"seq": lax.rem(me_seq + d, seqs)},
        )

    each(1, seqs, lambda d: to_seq(d).start())

    load_q[0].wait()
    for first in range(0, width, WIDE):
        q_snd[:, first : first + WIDE] = jnp.dot(
            x[...], wq[:, first : first + WIDE], preferred_element_type=F32
        ).astype(q_snd.dtype)
    send_q = to_core(q_snd, q_rcv, 1)
    send_q.start()
    load_q[1].wait()
    own = [
        jnp.dot(x[...], wq[:, width + first : width + first + WIDE], preferred_element_type=F32)
        for first in range(0, width, WIDE)
    ]
    send_q.wait_recv()
    for head in range(heads):
        at = head * HD
        summed = own[at // WIDE][:, at % WIDE : at % WIDE + HD] + q_rcv[:, at : at + HD].astype(F32)
        q[at : at + HD, :] = rotate(summed).astype(BF16)

    row_of = lax.broadcasted_iota(jnp.int32, (rows, 1), 0)
    lane_of = lax.broadcasted_iota(jnp.int32, (1, rows), 1)

    def positions(index, source):
        first, second = order_ref[2 * source] * half, order_ref[2 * source + 1] * half
        return jnp.where(index < half, first + index, second + (index - half))

    query_pos = positions(row_of, me_seq)

    def score(d):
        source = lax.rem(me_seq - d + seqs, seqs)
        visible = positions(lane_of, source) <= query_pos
        raw = lax.dot_general(
            q[...], kv[source, 0], (((1,), (1,)), ((), ())), preferred_element_type=F32
        )
        for head in range(heads):
            here = slice(head * rows, (head + 1) * rows)
            scores[source, here, :] = jnp.where(visible, raw[here], HIDDEN)

    score(0)

    def arrive(d):
        from_seq(d).wait_recv()
        score(d)

    each(1, seqs, arrive)

    stride = min(seqs, 4)
    best = scores[0]
    if seqs <= 8:
        for source in range(1, seqs):
            best = jnp.maximum(best, scores[source])
    else:
        best = lax.fori_loop(1, seqs, lambda s, b: jnp.maximum(b, scores[s]), best)
    top = jnp.max(best, axis=1, keepdims=True)
    factor = HD ** -0.5 * float(np.log2(np.e))

    def mix(index, carry):
        total, mixed = carry
        parts, values = [], []
        for inner in range(stride):
            source = index * stride + inner
            weights = jnp.exp2((scores[source] - top) * factor)
            total = total + weights
            parts.append(weights.astype(BF16))
            values.append(kv[source, 1])
        mixed = mixed + jnp.dot(
            jnp.concatenate(parts, axis=1), jnp.concatenate(values, axis=0),
            preferred_element_type=F32,
        )
        return total, mixed

    zero = jnp.zeros((heads * rows, HD), F32)
    if seqs <= 4:
        total, mixed = mix(0, (zero, zero))
    else:
        total, mixed = lax.fori_loop(0, seqs // stride, mix, (zero, zero))
    attended = (mixed / jnp.sum(total, axis=1, keepdims=True)).astype(BF16)
    for head in range(heads):
        att[:, head * HD : (head + 1) * HD] = attended[head * rows : (head + 1) * rows]
    send_att = to_core(att, att_peer, 2)
    send_att.start()

    steps = list(range(1, cols)) + [0]
    for step in steps:
        wo_load(step, 0).wait()
        partial_own[step] = jnp.dot(att[...], wo[step, :width, :], preferred_element_type=F32)
    send_att.wait_recv()

    def to_col(d):
        return pltpu.make_async_remote_copy(
            src_ref=rs_snd.at[d], dst_ref=rs_rcv.at[d],
            send_sem=col_send.at[d], recv_sem=col_recv.at[d],
            device_id={"col": lax.rem(me_col + d, cols)},
        )

    for step in steps:
        wo_load(step, 1).wait()
        summed = partial_own[step] + jnp.dot(
            att_peer[...], wo[step, width:, :], preferred_element_type=F32
        )
        if step == 0:
            partial_own[0] = summed
        else:
            rs_snd[step] = summed.astype(rs_snd.dtype)
            to_col(step).start()
    for d in range(1, cols):
        to_col(d).wait_recv()
    final = partial_own[0]
    for d in range(1, cols):
        final = final + rs_rcv[d].astype(F32)
    out_ref[...] = final

    send_kv.wait_send()
    send_q.wait_send()
    send_att.wait_send()
    each(1, seqs, lambda d: to_seq(d).wait_send())
    for d in range(1, cols):
        to_col(d).wait_send()


def body(seqs, cols, tokens, block_order, query_weight, key_weight, value_weight, output_weight):
    rows, depth = tokens.shape
    width = query_weight.shape[1] // 2
    out_width = output_weight.shape[1] // (2 * cols)
    heads = width // HD
    table = rotary_table(rows // 2, block_order.shape[0])
    anywhere = pl.BlockSpec(memory_space=pl.ANY)
    return pl.pallas_call(
        partial(layer_kernel, seqs, cols),
        out_shape=jax.ShapeDtypeStruct((rows, out_width), F32),
        in_specs=[pl.BlockSpec(memory_space=pltpu.SMEM)] + [anywhere] * 6,
        out_specs=pl.BlockSpec(memory_space=pltpu.VMEM),
        scratch_shapes=[
            pltpu.VMEM((rows, depth), BF16),
            pltpu.VMEM((depth, 4 * HD), BF16),
            pltpu.VMEM((depth, 2 * width), BF16),
            pltpu.VMEM((cols, 2 * width, out_width), BF16),
            pltpu.VMEM(table.shape, F32),
            pltpu.VMEM((2, rows, HD), F32),
            pltpu.VMEM((rows, 2 * HD), BF16),
            pltpu.VMEM((rows, 2 * HD), BF16),
            pltpu.VMEM((rows, width), BF16),
            pltpu.VMEM((rows, width), BF16),
            pltpu.VMEM((heads * rows, HD), BF16),
            pltpu.VMEM((seqs, 2, rows, HD), BF16),
            pltpu.VMEM((seqs, heads * rows, rows), F32),
            pltpu.VMEM((rows, width), BF16),
            pltpu.VMEM((rows, width), BF16),
            pltpu.VMEM((cols, rows, out_width), F32),
            pltpu.VMEM((cols, rows, out_width), BF16),
            pltpu.VMEM((cols, rows, out_width), BF16),
            pltpu.SemaphoreType.DMA((8,)),
            pltpu.SemaphoreType.DMA((cols, 2)),
            pltpu.SemaphoreType.DMA((3,)),
            pltpu.SemaphoreType.DMA((3,)),
            pltpu.SemaphoreType.DMA((seqs,)),
            pltpu.SemaphoreType.DMA((seqs,)),
            pltpu.SemaphoreType.DMA((cols,)),
            pltpu.SemaphoreType.DMA((cols,)),
        ],
        compiler_params=pltpu.CompilerParams(
            collective_id=0, has_side_effects=True, vmem_limit_bytes=48 * 2**20
        ),
    )(block_order, tokens, query_weight, key_weight, value_weight, output_weight, jnp.asarray(table))


def solution(mesh):
    placed = (
        P("seq", "row"),
        P(),
        P("row", "col"),
        P("row", "col"),
        P("row", "col"),
        P("col", None),
    )
    return jax.shard_map(
        partial(body, mesh.shape["seq"], mesh.shape["col"]),
        mesh=mesh, in_specs=placed, out_specs=P("seq", ("row", "col")), check_vma=False,
    )
```

time: 115 us -> 30.3 us (0.26)
  waiting for transfers between devices: 77.5 us -> 0 us
  Pallas kernels: 0 us -> 24.2 us
  between operations: 13.3 us -> 0.01 us
  matrix products: 12.4 us -> 0 us
  blocking collectives: 4.15 us -> 0 us
  local copies, waits for them, and re-layouts: 3.45 us -> 5.73 us
  other arithmetic: 2.07 us -> 0 us
  starting transfers between devices: 2 us -> 0 us
    reduce_scatter x2 -> x0, waiting for transfers between devices: 49.9 us -> none  [the longest x1 39.7 us: body(): lax.psum_scatter(partial_out, ('row', 'col'), scatter_dimension=1, tiled=...]
    pallas_call x0 -> x1, Pallas kernels: none -> 24.2 us  [body(): pl.pallas_call(partial(layer_kernel, seqs, cols), out_shape=jax.ShapeDtyp...]
    ppermute x3 -> x0, waiting for transfers between devices: 15.9 us -> none  [shifted(): lax.ppermute(array, axis, [(i, (i + by) % peers) for i in range(peers)])]
    dot_general x12 -> x0, matrix products: 12.4 us -> none  [the longest x1 4.3 us: body(): jnp.dot(attended, out_rows, preferred_element_type=jnp.float32)]
    psum x1 -> x0, waiting for transfers between devices: 11.7 us -> none  [body(): keys_summed, values_summed = lax.psum((keys_part, values_part), 'row')]
    unnamed x8 -> x11, local copies, waits for them, and re-layouts: 1.2 us -> 5.73 us
    psum x1 -> x0, blocking collectives: 4.15 us -> none  [body(): keys_summed, values_summed = lax.psum((keys_part, values_part), 'row')]
    ppermute x3 -> x0, starting transfers between devices: 1.88 us -> none  [shifted(): lax.ppermute(array, axis, [(i, (i + by) % peers) for i in range(peers)])]
  transfers between devices with their start and end apart: 6 -> 0, of which waited for: 6 -> 0; matrix products, arithmetic and copies ran while one was open for 6% -> 0% of each run, Pallas kernels for 0% -> 0%
where the time goes in v1:
time: 30.3 us; the launch traced here: 30 us
  Pallas kernels  24.2 us (80%)
  local copies, waits for them, and re-layouts  5.73 us (19%)
    pallas_call x1, Pallas kernels, body(): pl.pallas_call(partial(layer_kernel, seqs, cols), out_shape=jax.ShapeDtyp...  24.2 us
    unnamed x11, local copies, waits for them, and re-layouts  5.73 us

profile of v1, /device:TPU:0, one launch (start us, length us, event | category | flops | bytes accessed | tf_op | source)
XLA Modules:
  0.0 30.0 jit_solution(17095525616644833656)
XLA Ops:
  0.0 0.0 copy-start
  0.0 1.2 %copy-done = bf16[2048,256]{1,0:T(8,128)(2,1)S(1)} copy-done((bf16[2048,256]{1,0:T(8,128)(2,1)S(1)}, bf16[2048,256]{1,0:T(8,128)(2,1)}, u32[]{:S(2)}) %copy-start) | copy-done | bytes 1048600
  1.2 0.0 copy-start.1
  1.2 1.2 %copy-done.1 = bf16[2048,256]{1,0:T(8,128)(2,1)S(1)} copy-done((bf16[2048,256]{1,0:T(8,128)(2,1)S(1)}, bf16[2048,256]{1,0:T(8,128)(2,1)}, u32[]{:S(2)}) %copy-start.1) | copy-done | bytes 1048600
  2.5 0.0 copy-start.2
  2.5 1.0 %copy-done.2 = bf16[128,2048]{1,0:T(8,128)(2,1)S(1)} copy-done((bf16[128,2048]{1,0:T(8,128)(2,1)S(1)}, bf16[128,2048]{1,0:T(8,128)(2,1)}, u32[]{:S(2)}) %copy-start.2) | copy-done | bytes 524312
  3.5 0.0 copy-start.3
  3.5 0.9 %copy-done.3 = f32[72,256]{1,0:T(8,128)S(1)} copy-done((f32[72,256]{1,0:T(8,128)S(1)}, f32[72,256]{1,0:T(8,128)}, u32[]{:S(2)}) %copy-start.3) | copy-done | bytes 73752
  4.4 0.0 copy-start.4
  4.4 0.7 %copy-done.4 = s32[8]{0:T(128)S(1)} copy-done((s32[8]{0:T(128)S(1)}, s32[8]{0:T(128)}, u32[]{:S(2)}) %copy-start.4) | copy-done | bytes 56
  5.0 24.2 %shard_map.73 = f32[128,512]{1,0:T(8,128)S(1)} custom-call(s32[8]{0:T(128)S(1)} %copy-done.4, bf16[128,2048]{1,0:T(8,128)(2,1)S(1)} %copy-done.2, bf16[2048,1024]{1,0:T(8,128)(2,1)} %wq_hbm.1, bf16[2048,256]{1,0:T(8,128)(2,1)S(1)} %copy-done, bf16[2048,256]{1,0:T(8,128)(2,1)S(1)} %copy-done.1, bf16[1024,4096]{1,0:T(8,128)(2,1)} %wo_hbm.1, ...), custom_call_target="tpu_custom_call" | custom-call | tf_op jit(solution)/shard_map/pallas_call | solution.py:286
  29.3 0.7 %copy.9 = f32[128,512]{1,0:T(8,128)} copy(f32[128,512]{1,0:T(8,128)S(1)} %shard_map.73) | data formatting | bytes 524288
Async XLA Ops:
  0.0 1.2 %copy-start = (bf16[2048,256]{1,0:T(8,128)(2,1)S(1)}, bf16[2048,256]{1,0:T(8,128)(2,1)}, u32[]{:S(2)}) copy-start(bf16[2048,256]{1,0:T(8,128)(2,1)} %wk_hbm.1) | copy-start | bytes 3145732
  1.2 1.2 %copy-start.1 = (bf16[2048,256]{1,0:T(8,128)(2,1)S(1)}, bf16[2048,256]{1,0:T(8,128)(2,1)}, u32[]{:S(2)}) copy-start(bf16[2048,256]{1,0:T(8,128)(2,1)} %wv_hbm.1) | copy-start | bytes 3145732
  2.5 1.0 %copy-start.2 = (bf16[128,2048]{1,0:T(8,128)(2,1)S(1)}, bf16[128,2048]{1,0:T(8,128)(2,1)}, u32[]{:S(2)}) copy-start(bf16[128,2048]{1,0:T(8,128)(2,1)} %x_hbm.1) | copy-start | bytes 1572868
  3.5 0.9 %copy-start.3 = (f32[72,256]{1,0:T(8,128)S(1)}, f32[72,256]{1,0:T(8,128)}, u32[]{:S(2)}) copy-start(f32[72,256]{1,0:T(8,128)} %constant.2.clone.table_hbm) | copy-start | bytes 221188
  4.4 0.7 %copy-start.4 = (s32[8]{0:T(128)S(1)}, s32[8]{0:T(128)}, u32[]{:S(2)}) copy-start(s32[8]{0:T(128)} %order_ref.1) | copy-start | bytes 100

commit v2 on v1

v2 whole, which is shorter than its diff:
```python
from functools import partial

import jax
import jax.numpy as jnp
import numpy as np
from jax import lax
from jax.experimental import pallas as pl
from jax.experimental.pallas import tpu as pltpu
from jax.sharding import PartitionSpec as P

H = 32
KV = 8
HD = 128
THETA = 500000.0
HIDDEN = -1e30
WIDE = 256
F32 = jnp.float32
BF16 = jnp.bfloat16


def rotary_table(half_rows, blocks):
    freqs = THETA ** (-2.0 * np.arange(HD // 2) / HD)
    starts = np.concatenate([np.arange(half_rows), half_rows * np.arange(blocks)])
    angles = starts[:, None] * freqs[None, :]
    cosine, sine = np.cos(angles), np.sin(angles)
    return np.concatenate([cosine, cosine, -sine, sine], axis=1).astype(np.float32)


def flip(index, mask):
    for bit in range(mask.bit_length()):
        if mask >> bit & 1:
            index = index + (1 - 2 * (index // 2**bit % 2)) * 2**bit
    return index


def each(first, last, step):
    if last - first <= 8:
        for index in range(first, last):
            step(index)
    else:
        lax.fori_loop(first, last, lambda index, _: (step(index), 0)[1], 0)


def layer_kernel(
    seqs, cols,
    order_ref, x_hbm, wq_hbm, wk_hbm, wv_hbm, wo_hbm, table_hbm,
    out_ref,
    x, wkv, wq, wo, table, rot,
    kv_snd, kv_rcv, q_snd, q_rcv, q, kv, att, att_peer, partial_own, rs_snd, rs_rcv,
    load_sem, wo_sem, core_send, core_recv, seq_send, seq_recv, col_send, col_recv,
):
    rows = x.shape[0]
    half = rows // 2
    heads = wq.shape[1] // 2 // HD
    width = heads * HD
    group = H // KV
    out_width = wo.shape[2]

    me_seq = lax.axis_index("seq")
    me_row = lax.axis_index("row")
    me_col = lax.axis_index("col")
    other = 1 - me_row

    def kv_columns(row):
        return pl.ds(pl.multiple_of(row * heads // group * HD, HD), HD)

    def q_columns(row):
        return pl.ds(pl.multiple_of(row * width, width), width)

    loads = [pltpu.make_async_copy(x_hbm, x, load_sem.at[0])]
    for slot, (source, row) in enumerate(
        [(wk_hbm, other), (wv_hbm, other), (wk_hbm, me_row), (wv_hbm, me_row)]
    ):
        loads.append(
            pltpu.make_async_copy(
                source.at[:, kv_columns(row)],
                wkv.at[:, pl.ds(slot * HD, HD)],
                load_sem.at[1 + slot],
            )
        )
    loads.append(pltpu.make_async_copy(table_hbm, table, load_sem.at[7]))
    for slot, row in enumerate([other, me_row]):
        loads.append(
            pltpu.make_async_copy(
                wq_hbm.at[:, q_columns(row)],
                wq.at[:, pl.ds(slot * width, width)],
                load_sem.at[5 + slot],
            )
        )
    for load in loads:
        load.start()
    load_x, load_kv, load_table, load_q = loads[0], loads[1:5], loads[5], loads[6:]

    def wo_load(step, part):
        target = flip(me_col, step)
        row = me_row if part == 0 else other
        first = pl.multiple_of((me_row * cols + target) * out_width, out_width)
        return pltpu.make_async_copy(
            wo_hbm.at[q_columns(row), pl.ds(first, out_width)],
            wo.at[step, pl.ds(part * width, width), :],
            wo_sem.at[step, part],
        )

    for part in range(2):
        for step in list(range(cols - 1, -1, -1)):
            wo_load(step, part).start()

    barrier = pltpu.get_barrier_semaphore()
    pl.semaphore_signal(barrier, inc=1, device_id={"row": other})
    each(1, seqs, lambda d: pl.semaphore_signal(
        barrier, inc=1, device_id={"seq": lax.rem(me_seq + d, seqs)}))
    each(1, cols, lambda d: pl.semaphore_signal(
        barrier, inc=1, device_id={"col": lax.rem(me_col + d, cols)}))

    load_table.wait()
    for part in range(2):
        cos_in = table[0:half, 0:HD]
        sin_in = table[0:half, HD:]
        start = table[pl.ds(half + order_ref[2 * me_seq + part], 1), :]
        cos_at, sin_at = start[:, :HD], start[:, HD:]
        here = pl.ds(part * half, half)
        rot[0, here, :] = cos_at * cos_in - sin_at * sin_in
        rot[1, here, :] = sin_at * cos_in + cos_at * sin_in

    def rotate(vectors, here):
        return vectors * rot[0, here] + pltpu.roll(vectors, HD // 2, 1) * rot[1, here]

    halves = [slice(0, half), slice(half, rows)]

    def to_core(source, target, index):
        return pltpu.make_async_remote_copy(
            src_ref=source, dst_ref=target,
            send_sem=core_send.at[index], recv_sem=core_recv.at[index],
            device_id={"row": other},
        )

    load_x.wait()
    load_kv[0].wait()
    load_kv[1].wait()
    kv_snd[...] = jnp.dot(x[...], wkv[:, : 2 * HD], preferred_element_type=F32).astype(kv_snd.dtype)
    pl.semaphore_wait(barrier, 1 + (seqs - 1) + (cols - 1))
    send_kv = to_core(kv_snd, kv_rcv, 0)
    send_kv.start()
    load_kv[2].wait()
    load_kv[3].wait()
    kv_own = jnp.dot(x[...], wkv[:, 2 * HD :], preferred_element_type=F32)
    send_kv.wait_recv()

    def seq_copy(part, d, source):
        return pltpu.make_async_remote_copy(
            src_ref=kv.at[source, part], dst_ref=kv.at[source, part],
            send_sem=seq_send.at[part, d], recv_sem=seq_recv.at[part, d],
            device_id={"seq": lax.rem(me_seq + d, seqs)},
        )

    def to_seq(part, d):
        return seq_copy(part, d, me_seq)

    def from_seq(part, d):
        return seq_copy(part, d, lax.rem(me_seq - d + seqs, seqs))

    for part, here in enumerate(halves):
        kv_sum = kv_own[here] + kv_rcv[here, :].astype(F32)
        kv[me_seq, part, 0] = rotate(kv_sum[:, :HD], here).astype(BF16)
        kv[me_seq, part, 1] = kv_sum[:, HD:].astype(BF16)
        each(1, seqs, lambda d: to_seq(part, d).start())

    load_q[0].wait()
    for first in range(0, width, WIDE):
        q_snd[:, first : first + WIDE] = jnp.dot(
            x[...], wq[:, first : first + WIDE], preferred_element_type=F32
        ).astype(q_snd.dtype)
    send_q = to_core(q_snd, q_rcv, 1)
    send_q.start()
    load_q[1].wait()
    own = [
        jnp.dot(x[...], wq[:, width + first : width + first + WIDE], preferred_element_type=F32)
        for first in range(0, width, WIDE)
    ]
    send_q.wait_recv()
    for head in range(heads):
        at = head * HD
        summed = own[at // WIDE][:, at % WIDE : at % WIDE + HD] + q_rcv[:, at : at + HD].astype(F32)
        for part, here in enumerate(halves):
            q[part, head * half : (head + 1) * half, :] = rotate(summed[here], here).astype(BF16)

    stride = 4 if seqs % 4 == 0 else 1
    factor = HD ** -0.5 * float(np.log2(np.e))
    lane = lax.broadcasted_iota(jnp.int32, (1, stride * half), 1)
    row = lax.rem(lax.broadcasted_iota(jnp.int32, (heads * half, 1), 0), half)

    def attend(part, key_part, index, state):
        first = index * stride
        keys = jnp.concatenate([kv[first + i, key_part, 0] for i in range(stride)], axis=0)
        values = jnp.concatenate([kv[first + i, key_part, 1] for i in range(stride)], axis=0)
        scores = lax.dot_general(
            q[part], keys, (((1,), (1,)), ((), ())), preferred_element_type=F32
        )
        if part == key_part:
            key_pos = order_ref[2 * first + part] * half + lane
            for i in range(1, stride):
                start = order_ref[2 * (first + i) + part] * half
                key_pos = jnp.where(lane >= i * half, start + lane - i * half, key_pos)
            visible = key_pos <= order_ref[2 * me_seq + part] * half + row
            scores = jnp.where(visible, scores, HIDDEN)
        top = jnp.max(scores, axis=1, keepdims=True)
        if state is not None:
            top = jnp.maximum(top, state[0])
        weights = jnp.exp2((scores - top) * factor)
        if part == key_part:
            weights = jnp.where(visible, weights, 0.0)
        total = jnp.sum(weights, axis=1, keepdims=True)
        mixed = jnp.dot(weights.astype(BF16), values, preferred_element_type=F32)
        if state is not None:
            rescale = jnp.exp2((state[0] - top) * factor)
            total = total + state[1] * rescale
            mixed = mixed + state[2] * rescale
        return top, total, mixed

    def attend_all(part, key_part, state):
        if seqs == stride:
            return attend(part, key_part, 0, state)
        if state is None:
            state = (
                jnp.full((heads * half, 1), HIDDEN, F32),
                jnp.zeros((heads * half, 1), F32),
                jnp.zeros((heads * half, HD), F32),
            )
        return lax.fori_loop(0, seqs // stride, partial(attend, part, key_part), state)

    def send_attended(part, state):
        attended = (state[2] / state[1]).astype(BF16)
        for head in range(heads):
            att[part, :, head * HD : (head + 1) * HD] = attended[head * half : (head + 1) * half]
        att_copy(part).start()

    def att_copy(part):
        return to_core(att.at[part], att_peer.at[part], 2 + part)

    steps = list(range(cols - 1, -1, -1))

    def to_col(part, d):
        return pltpu.make_async_remote_copy(
            src_ref=rs_snd.at[d, part], dst_ref=rs_rcv.at[d, part],
            send_sem=col_send.at[d, part], recv_sem=col_recv.at[d, part],
            device_id={"col": flip(me_col, d)},
        )

    def own_sums(part):
        for step in steps:
            if part == 0:
                wo_load(step, 0).wait()
            partial_own[step, part] = jnp.dot(
                att[part], wo[step, :width, :], preferred_element_type=F32
            )

    def send_sums(part):
        att_copy(part).wait_recv()
        for step in steps:
            if part == 0:
                wo_load(step, 1).wait()
            summed = partial_own[step, part] + jnp.dot(
                att_peer[part], wo[step, width:, :], preferred_element_type=F32
            )
            if step == 0:
                partial_own[0, part] = summed
            else:
                rs_snd[step, part] = summed.astype(rs_snd.dtype)
                to_col(part, step).start()

    def finish(part):
        final = partial_own[0, part]
        for d in range(1, cols):
            to_col(part, d).wait_recv()
            final = final + rs_rcv[d, part].astype(F32)
        out_ref[halves[part], :] = final

    each(1, seqs, lambda d: from_seq(0, d).wait_recv())
    send_attended(0, attend_all(0, 0, None))
    own_sums(0)
    upper = attend_all(1, 0, None)
    send_sums(0)
    each(1, seqs, lambda d: from_seq(1, d).wait_recv())
    send_attended(1, attend_all(1, 1, upper))
    own_sums(1)
    send_sums(1)
    finish(0)
    finish(1)

    send_kv.wait_send()
    send_q.wait_send()
    for part in range(2):
        att_copy(part).wait_send()
        each(1, seqs, lambda d: to_seq(part, d).wait_send())
        for d in range(1, cols):
            to_col(part, d).wait_send()


def body(seqs, cols, tokens, block_order, query_weight, key_weight, value_weight, output_weight):
    rows, depth = tokens.shape
    width = query_weight.shape[1] // 2
    out_width = output_weight.shape[1] // (2 * cols)
    heads = width // HD
    table = rotary_table(rows // 2, block_order.shape[0])
    anywhere = pl.BlockSpec(memory_space=pl.ANY)
    return pl.pallas_call(
        partial(layer_kernel, seqs, cols),
        out_shape=pltpu.VMEM((rows, out_width), F32),
        in_specs=[pl.BlockSpec(memory_space=pltpu.SMEM)] + [anywhere] * 6,
        out_specs=pl.BlockSpec(memory_space=pltpu.VMEM),
        scratch_shapes=[
            pltpu.VMEM((rows, depth), BF16),
            pltpu.VMEM((depth, 4 * HD), BF16),
            pltpu.VMEM((depth, 2 * width), BF16),
            pltpu.VMEM((cols, 2 * width, out_width), BF16),
            pltpu.VMEM(table.shape, F32),
            pltpu.VMEM((2, rows, HD), F32),
            pltpu.VMEM((rows, 2 * HD), BF16),
            pltpu.VMEM((rows, 2 * HD), BF16),
            pltpu.VMEM((rows, width), BF16),
            pltpu.VMEM((rows, width), BF16),
            pltpu.VMEM((2, heads * rows // 2, HD), BF16),
            pltpu.VMEM((seqs, 2, 2, rows // 2, HD), BF16),
            pltpu.VMEM((2, rows // 2, width), BF16),
            pltpu.VMEM((2, rows // 2, width), BF16),
            pltpu.VMEM((cols, 2, rows // 2, out_width), F32),
            pltpu.VMEM((cols, 2, rows // 2, out_width), BF16),
            pltpu.VMEM((cols, 2, rows // 2, out_width), BF16),
            pltpu.SemaphoreType.DMA((8,)),
            pltpu.SemaphoreType.DMA((cols, 2)),
            pltpu.SemaphoreType.DMA((4,)),
            pltpu.SemaphoreType.DMA((4,)),
            pltpu.SemaphoreType.DMA((2, seqs)),
            pltpu.SemaphoreType.DMA((2, seqs)),
            pltpu.SemaphoreType.DMA((cols, 2)),
            pltpu.SemaphoreType.DMA((cols, 2)),
        ],
        compiler_params=pltpu.CompilerParams(
            collective_id=0, has_side_effects=True, vmem_limit_bytes=60 * 2**20
        ),
    )(block_order, tokens, query_weight, key_weight, value_weight, output_weight, jnp.asarray(table))


def solution(mesh):
    placed = (
        P("seq", "row"),
        P(),
        P("row", "col"),
        P("row", "col"),
        P("row", "col"),
        P("col", None),
    )
    return jax.shard_map(
        partial(body, mesh.shape["seq"], mesh.shape["col"]),
        mesh=mesh, in_specs=placed, out_specs=P("seq", ("row", "col")), check_vma=False,
    )
```

time: 30.3 us -> 23.6 us (0.78)
  local copies, waits for them, and re-layouts: 5.73 us -> 0.71 us
  Pallas kernels: 24.2 us -> 22.7 us
    unnamed x11 -> x1, local copies, waits for them, and re-layouts: 5.73 us -> 0.71 us
    pallas_call x1, Pallas kernels: 24.2 us -> 22.7 us  [body(): pl.pallas_call(partial(layer_kernel, seqs, cols), out_shape=pltpu.VMEM((r...]
where the time goes in v2:
time: 23.6 us; the launch traced here: 23.4 us
  Pallas kernels  22.7 us (96%)
  local copies, waits for them, and re-layouts  0.71 us (3%)
    pallas_call x1, Pallas kernels, body(): pl.pallas_call(partial(layer_kernel, seqs, cols), out_shape=pltpu.VMEM((r...  22.7 us
    unnamed x1, local copies, waits for them, and re-layouts  0.71 us

profile of v2, /device:TPU:0, one launch (start us, length us, event | category | flops | bytes accessed | tf_op | source)
XLA Modules:
  0.0 23.4 jit_solution(5118663419628855189)
XLA Ops:
  0.0 22.7 %shard_map.73 = f32[128,512]{1,0:T(8,128)S(1)} custom-call(s32[8]{0:T(128)} %order_ref.1, bf16[128,2048]{1,0:T(8,128)(2,1)} %x_hbm.1, bf16[2048,1024]{1,0:T(8,128)(2,1)} %wq_hbm.1, bf16[2048,256]{1,0:T(8,128)(2,1)} %wk_hbm.1, bf16[2048,256]{1,0:T(8,128)(2,1)} %wv_hbm.1, bf16[1024,4096]{1,0:T(8,128)(2,1)} %wo_hbm.1, f32[72,256]{1,0:T(8,128)} %constant.2.clone.table_hbm), custom_call_target="tpu_custom_call" | custom-call | tf_op jit(solution)/shard_map/pallas_call | solution.py:306
  22.7 0.7 %copy.9 = f32[128,512]{1,0:T(8,128)} copy(f32[128,512]{1,0:T(8,128)S(1)} %shard_map.73) | data formatting | bytes 524288

commit v3 on v2

--- a/solution.py
+++ b/solution.py
@@ -43,11 +43,11 @@
 
 def layer_kernel(
     seqs, cols,
-    order_ref, x_hbm, wq_hbm, wk_hbm, wv_hbm, wo_hbm, table_hbm,
+    order_hbm, x_hbm, wq_hbm, wk_hbm, wv_hbm, wo_hbm, table_hbm,
     out_ref,
     x, wkv, wq, wo, table, rot,
     kv_snd, kv_rcv, q_snd, q_rcv, q, kv, att, att_peer, partial_own, rs_snd, rs_rcv,
-    load_sem, wo_sem, core_send, core_recv, seq_send, seq_recv, col_send, col_recv,
+    order_ref, load_sem, wo_sem, core_send, core_recv, seq_send, seq_recv, col_send, col_recv,
 ):
     rows = x.shape[0]
     half = rows // 2
@@ -66,6 +66,13 @@
 
     def q_columns(row):
         return pl.ds(pl.multiple_of(row * width, width), width)
+
+    barrier = pltpu.get_barrier_semaphore()
+    pl.semaphore_signal(barrier, inc=1, device_id={"row": other})
+    each(1, seqs, lambda d: pl.semaphore_signal(
+        barrier, inc=1, device_id={"seq": lax.rem(me_seq + d, seqs)}))
+    each(1, cols, lambda d: pl.semaphore_signal(
+        barrier, inc=1, device_id={"col": lax.rem(me_col + d, cols)}))
 
     loads = [pltpu.make_async_copy(x_hbm, x, load_sem.at[0])]
     for slot, (source, row) in enumerate(
@@ -89,6 +96,8 @@
         )
     for load in loads:
         load.start()
+    load_order = pltpu.make_async_copy(order_hbm, order_ref, load_sem.at[8])
+    load_order.start()
     load_x, load_kv, load_table, load_q = loads[0], loads[1:5], loads[5], loads[6:]
 
     def wo_load(step, part):
@@ -105,14 +114,8 @@
         for step in list(range(cols - 1, -1, -1)):
             wo_load(step, part).start()
 
-    barrier = pltpu.get_barrier_semaphore()
-    pl.semaphore_signal(barrier, inc=1, device_id={"row": other})
-    each(1, seqs, lambda d: pl.semaphore_signal(
-        barrier, inc=1, device_id={"seq": lax.rem(me_seq + d, seqs)}))
-    each(1, cols, lambda d: pl.semaphore_signal(
-        barrier, inc=1, device_id={"col": lax.rem(me_col + d, cols)}))
-
     load_table.wait()
+    load_order.wait()
     for part in range(2):
         cos_in = table[0:half, 0:HD]
         sin_in = table[0:half, HD:]
@@ -306,7 +309,7 @@
     return pl.pallas_call(
         partial(layer_kernel, seqs, cols),
         out_shape=pltpu.VMEM((rows, out_width), F32),
-        in_specs=[pl.BlockSpec(memory_space=pltpu.SMEM)] + [anywhere] * 6,
+        in_specs=[anywhere] * 7,
         out_specs=pl.BlockSpec(memory_space=pltpu.VMEM),
         scratch_shapes=[
             pltpu.VMEM((rows, depth), BF16),
@@ -326,7 +329,8 @@
             pltpu.VMEM((cols, 2, rows // 2, out_width), F32),
             pltpu.VMEM((cols, 2, rows // 2, out_width), BF16),
             pltpu.VMEM((cols, 2, rows // 2, out_width), BF16),
-            pltpu.SemaphoreType.DMA((8,)),
+            pltpu.SMEM(block_order.shape, jnp.int32),
+            pltpu.SemaphoreType.DMA((9,)),
             pltpu.SemaphoreType.DMA((cols, 2)),
             pltpu.SemaphoreType.DMA((4,)),
             pltpu.SemaphoreType.DMA((4,)),

time: 23.6 us -> 22.8 us (0.966)
  Pallas kernels: 22.7 us -> 21.9 us
    pallas_call x1, Pallas kernels: 22.7 us -> 21.9 us  [body(): pl.pallas_call(partial(layer_kernel, seqs, cols), out_shape=pltpu.VMEM((r...]
where the time goes in v3:
time: 22.8 us; the launch traced here: 22.6 us
  Pallas kernels  21.9 us (96%)
  local copies, waits for them, and re-layouts  0.71 us (3%)
    pallas_call x1, Pallas kernels, body(): pl.pallas_call(partial(layer_kernel, seqs, cols), out_shape=pltpu.VMEM((r...  21.9 us
    unnamed x1, local copies, waits for them, and re-layouts  0.71 us

profile of v3, /device:TPU:0, one launch (start us, length us, event | category | flops | bytes accessed | tf_op | source)
XLA Modules:
  0.0 22.6 jit_solution(10865534638756811471)
XLA Ops:
  0.0 21.9 %shard_map.73 = f32[128,512]{1,0:T(8,128)S(1)} custom-call(s32[8]{0:T(128)} %order_hbm.1, bf16[128,2048]{1,0:T(8,128)(2,1)} %x_hbm.1, bf16[2048,1024]{1,0:T(8,128)(2,1)} %wq_hbm.1, bf16[2048,256]{1,0:T(8,128)(2,1)} %wk_hbm.1, bf16[2048,256]{1,0:T(8,128)(2,1)} %wv_hbm.1, bf16[1024,4096]{1,0:T(8,128)(2,1)} %wo_hbm.1, f32[72,256]{1,0:T(8,128)} %constant.2.clone.table_hbm), custom_call_target="tpu_custom_call" | custom-call | tf_op jit(solution)/shard_map/pallas_call | solution.py:309
  21.9 0.7 %copy.9 = f32[128,512]{1,0:T(8,128)} copy(f32[128,512]{1,0:T(8,128)S(1)} %shard_map.73) | data formatting | bytes 524288
